TPU v7x, 512 devices: a whole 4x4x16 slice. The times are simulated.
512 devices in a mesh: expert: 32 (over y, x, z_hi), tensor: 16 (over z_lo, core).
Axes of the slice: x: 4, y: 4, z: 16 (z_hi: 2, z_lo: 8; z = z_hi * 8 + z_lo), core: 2. Of those that a mesh axis runs over, the one named last changes fastest.
Arguments:
- tokens: bfloat16 [4096, 2560], P('expert', 'tensor'), may hold values from -6 to 6
- first_gain: float32 [2560], replicated, may hold values from 0.1 to 1.9
- dense_gate: bfloat16 [2560, 8192], P('expert', 'tensor'), may hold values from -0.125 to 0.125
- dense_up: bfloat16 [2560, 8192], P('expert', 'tensor'), may hold values from -0.125 to 0.125
- dense_down: bfloat16 [2560, 8192], P('expert', 'tensor'), may hold values from -0.0625 to 0.0625
- second_gain: float32 [2560], replicated, may hold values from 0.1 to 1.9
- shared_gate: bfloat16 [2560, 4096], P('expert', 'tensor'), may hold values from -0.125 to 0.125
- shared_up: bfloat16 [2560, 4096], P('expert', 'tensor'), may hold values from -0.125 to 0.125
- shared_down: bfloat16 [2560, 4096], P('expert', 'tensor'), may hold values from -0.09375 to 0.09375
- expert_gate: bfloat16 [32, 2560, 4096], P('expert', None, 'tensor'), may hold values from -0.125 to 0.125
- expert_up: bfloat16 [32, 2560, 4096], P('expert', None, 'tensor'), may hold values from -0.125 to 0.125
- expert_down: bfloat16 [32, 2560, 4096], P('expert', None, 'tensor'), may hold values from -0.09375 to 0.09375
- routes: int32 [4096, 1], P('expert'), may hold values from 0 to 31; in each aligned block of 128 rows (0 to 127, 128 to 255, ...) at most 8 rows name the same one
- route_gate: float32 [4096, 1], P('expert'), may hold values from 0.25 to 1
Outputs:
- mixed: bfloat16 [4096, 2560], P('expert', 'tensor')
Inputs may be any that keep to these rules, and one draw needn't show every extreme that they name: `routes`: within each aligned block of 128 tokens (the tokens of one index of expert), no expert is named by more than 8 tokens, and that number is reached in some block.
All inputs are finite; a program needn't handle non-finite values.
Results may differ from a plain program's by a relative error of at most 0.025.
Values may be sent and summed in bfloat16 or wider, within the bound.
A program may use at most 64 MiB of HBM per device.

v0:
```python
import jax
import jax.numpy as jnp
from jax import lax
from jax.sharding import PartitionSpec as P

EPSILON = 1e-05


def rms_scaled(rows, gain):
    wide_rows = rows.astype(jnp.float32)
    square_mean = jnp.mean(wide_rows * wide_rows, axis=1, keepdims=True)
    return (wide_rows * lax.rsqrt(square_mean + EPSILON) * gain).astype(jnp.bfloat16)


def ffn_partial(normed, gate_rows, up_rows, down_rows):
    gate_part = jnp.dot(
        normed,
        lax.all_gather(gate_rows, "expert", axis=0, tiled=True),
        preferred_element_type=jnp.float32,
    )
    up_part = jnp.dot(
        normed,
        lax.all_gather(up_rows, "expert", axis=0, tiled=True),
        preferred_element_type=jnp.float32,
    )
    hidden = (jax.nn.silu(gate_part) * up_part).astype(jnp.bfloat16)
    return lax.dot_general(
        hidden,
        lax.all_gather(down_rows, "expert", axis=0, tiled=True),
        (((1,), (1,)), ((), ())),
        preferred_element_type=jnp.float32,
    )


def tensor_total(partial_value, residual, keep_whole):
    col_width = partial_value.shape[1] // lax.axis_size("tensor")
    offset = lax.axis_index("tensor") * col_width
    summed = lax.psum(partial_value.astype(jnp.bfloat16), "tensor").astype(jnp.float32)
    total = (residual.astype(jnp.float32) + summed).astype(jnp.bfloat16)
    if keep_whole:
        return total
    return lax.dynamic_slice_in_dim(total, offset, col_width, 1)


def slot_table(routes, experts, slot_depth):
    matches = (routes == jnp.arange(experts, dtype=jnp.int32)[None, :]).astype(jnp.int32)
    earlier = jnp.cumsum(matches, axis=0) - matches
    slot_rank = jnp.sum(earlier * matches, axis=1)
    slot_index = routes[:, 0] * slot_depth + slot_rank
    return (
        slot_index[:, None] == jnp.arange(experts * slot_depth, dtype=jnp.int32)[None, :]
    ).astype(jnp.bfloat16)


def local(
    tokens,
    first_gain,
    dense_gate,
    dense_up,
    dense_down,
    second_gain,
    shared_gate,
    shared_up,
    shared_down,
    expert_gate,
    expert_up,
    expert_down,
    routes,
    route_gate,
):
    full_tokens = lax.all_gather(tokens, "tensor", axis=1, tiled=True)
    first_normed = rms_scaled(full_tokens, first_gain)
    dense_part = ffn_partial(first_normed, dense_gate, dense_up, dense_down)
    middle = tensor_total(dense_part, full_tokens, True)
    second_normed = rms_scaled(middle, second_gain)
    experts = lax.axis_size("expert")
    feature_count = full_tokens.shape[1]
    slot_depth = 2 * full_tokens.shape[0] // experts
    onehot = slot_table(routes, experts, slot_depth)
    gathered = lax.dot_general(
        onehot, second_normed, (((0,), (0,)), ((), ())), preferred_element_type=jnp.float32
    )
    full_rows = lax.all_to_all(
        gathered.astype(jnp.bfloat16).reshape(experts, slot_depth, second_normed.shape[1]),
        "expert",
        split_axis=0,
        concat_axis=0,
        tiled=True,
    )
    source_count, slot_count, _ = full_rows.shape
    flat_rows = full_rows.reshape(source_count * slot_count, feature_count)
    gate_part = jnp.dot(flat_rows, expert_gate[0], preferred_element_type=jnp.float32)
    up_part = jnp.dot(flat_rows, expert_up[0], preferred_element_type=jnp.float32)
    hidden = (jax.nn.silu(gate_part) * up_part).astype(jnp.bfloat16)
    expert_out = lax.dot_general(
        hidden, expert_down[0], (((1,), (1,)), ((), ())), preferred_element_type=jnp.float32
    )
    expert_out = expert_out.astype(jnp.bfloat16).reshape(source_count, slot_count, feature_count)
    returned = lax.all_to_all(expert_out, "expert", split_axis=0, concat_axis=0, tiled=True)
    shared_part = ffn_partial(second_normed, shared_gate, shared_up, shared_down)
    routed = jnp.dot(
        onehot,
        returned.reshape(experts * slot_depth, feature_count),
        preferred_element_type=jnp.float32,
    )
    device_term = shared_part + route_gate * routed
    return tensor_total(device_term, middle, False)


def solution(mesh):
    placed = (
        P("expert", "tensor"),
        P(),
        P("expert", "tensor"),
        P("expert", "tensor"),
        P("expert", "tensor"),
        P(),
        P("expert", "tensor"),
        P("expert", "tensor"),
        P("expert", "tensor"),
        P("expert", None, "tensor"),
        P("expert", None, "tensor"),
        P("expert", None, "tensor"),
        P("expert", None),
        P("expert", None),
    )
    return jax.shard_map(
        local, mesh=mesh, in_specs=placed, out_specs=P("expert", "tensor"), check_vma=False
    )
```

profile of v0, /device:TPU:1, one launch (start us, length us, event | category | flops | bytes accessed | tf_op | source)
XLA Modules:
  0.0 1234.6 jit_solution(16643097461971188907)
XLA Ops:
  6.5 0.7 all-gather.7.cloned.1.call-update
  7.3 0.0 all-gather.11.cloned.1.call-start
  7.3 0.7 all-gather.11.cloned.1.call-update
  8.0 0.0 all-gather.9.cloned.1.call-start
  8.1 0.7 all-gather.9.cloned.1.call-update
  8.7 0.0 copy-start.2
  8.8 0.0 all-reduce.3.cloned.1.call-start
  8.8 41.5 %all_gather.21 = bf16[128,2560]{0,1:T(8,128)(2,1)S(1)} all-gather(bf16[128,160]{0,1:T(8,128)(2,1)} %param.14), channel_id=1, replica_groups=mesh['expert'=32,'tensor'=16] {'tensor'}, dimensions={1}, use_global_device_ids=true | all-gather | bytes 696320 | tf_op jit(solution)/shard_map/all_gather | solution.py:71
  50.3 0.2 copy.19
  50.5 0.2 fusion.3
  50.8 103.4 %all-gather.7.cloned.1.call-done = bf16[2560,512]{1,0:T(8,128)(2,1)} async-done(((bf16[80,512]{1,0:T(8,128)(2,1)}), bf16[2560,512]{1,0:T(8,128)(2,1)}) %all-gather.7.cloned.1.call-update) | async-done | bytes 2621456 | tf_op jit(solution)/shard_map/all_gather | solution.py:18
  154.1 2.3 fusion.44
  156.4 0.0 copy-start.4
  156.4 133.3 %all-gather.11.cloned.1.call-done = bf16[2560,512]{1,0:T(8,128)(2,1)} async-done(((bf16[80,512]{1,0:T(8,128)(2,1)}), bf16[2560,512]{1,0:T(8,128)(2,1)}) %all-gather.11.cloned.1.call-update) | async-done | bytes 2621456 | tf_op jit(solution)/shard_map/all_gather | solution.py:29
  289.7 135.6 %all-gather.9.cloned.1.call-done = bf16[2560,512]{1,0:T(8,128)(2,1)} async-done(((bf16[80,512]{1,0:T(8,128)(2,1)}), bf16[2560,512]{1,0:T(8,128)(2,1)}) %all-gather.9.cloned.1.call-update) | async-done | bytes 2621456 | tf_op jit(solution)/shard_map/all_gather | solution.py:23
  425.3 4.8 convolution_convert_fusion.2
  430.1 0.0 all-reduce.3.cloned.1.call-update
  430.2 0.1 fusion.56
  430.2 0.2 reduce_window_sum.11
  430.4 0.2 select_reduce_fusion
  430.6 191.9 %all-reduce.3.cloned.1.call-done = bf16[128,2560]{1,0:T(8,128)(2,1)} async-done(((bf16[128,2560]{1,0:T(8,128)(2,1)}), bf16[128,2560]{1,0:T(8,128)(2,1)}) %all-reduce.3.cloned.1.call-update) | async-done | bytes 655376 | tf_op jit(solution)/shard_map/psum | solution.py:38
  622.5 1.4 multiply_reduce_fusion
  623.9 1.3 multiply_convert_fusion
  625.3 1.7 fusion
  627.0 9.4 all-to-all-start
  636.4 0.0 all-gather.13.cloned.1.call-start
  636.5 0.5 all-gather.13.cloned.1.call-update
  637.0 52.1 %all-to-all-done = bf16[32,8,2560]{2,1,0:T(8,128)(2,1)S(1)} async-done(((bf16[32,8,2560]{2,1,0:T(8,128)(2,1)}), bf16[32,8,2560]{2,1,0:T(8,128)(2,1)S(1)}, u32[]{:S(2)}, u32[]{:S(2)}) %all-to-all-start) | async-done | bytes 1310752 | tf_op jit(solution)/shard_map/all_to_all | solution.py:83
  689.1 1.8 fusion.11
  690.9 4.0 fusion.1
  694.9 51.7 %all-to-all-start.1 = ((bf16[32,8,2560]{2,1,0:T(8,128)(2,1)}), bf16[32,8,2560]{2,1,0:T(8,128)(2,1)S(1)}, u32[]{:S(2)}, u32[]{:S(2)}) async-start(bf16[32,8,2560]{2,1,0:T(8,128)(2,1)} %fusion.1), calls=%async_computation.1 | async-start | bytes 2621440 | tf_op jit(solution)/shard_map/all_to_all | solution.py:99
  746.6 0.0 copy-start.5
  746.6 0.0 all-gather.15.cloned.1.call-start
  746.7 0.5 all-gather.15.cloned.1.call-update
  747.2 0.0 all-gather.17.cloned.1.call-start
  747.2 0.7 all-gather.17.cloned.1.call-update
  747.9 0.0 all-reduce.5.cloned.1.call-start
  748.0 63.7 %all-gather.13.cloned.1.call-done = bf16[2560,256]{1,0:T(8,128)(2,1)} async-done(((bf16[80,256]{1,0:T(8,128)(2,1)}), bf16[2560,256]{1,0:T(8,128)(2,1)}) %all-gather.13.cloned.1.call-update) | async-done | bytes 1310736 | tf_op jit(solution)/shard_map/all_gather | solution.py:18
  811.7 1.7 fusion.62
  813.3 0.0 all-to-all-done.1
  813.4 1.4 convolution_multiply_fusion
  814.8 107.7 %all-gather.15.cloned.1.call-done = bf16[2560,256]{1,0:T(8,128)(2,1)} async-done(((bf16[80,256]{1,0:T(8,128)(2,1)}), bf16[2560,256]{1,0:T(8,128)(2,1)}) %all-gather.15.cloned.1.call-update) | async-done | bytes 1310736 | tf_op jit(solution)/shard_map/all_gather | solution.py:23
  922.5 110.9 %all-gather.17.cloned.1.call-done = bf16[2560,256]{1,0:T(8,128)(2,1)} async-done(((bf16[80,256]{1,0:T(8,128)(2,1)}), bf16[2560,256]{1,0:T(8,128)(2,1)}) %all-gather.17.cloned.1.call-update) | async-done | bytes 1310736 | tf_op jit(solution)/shard_map/all_gather | solution.py:29
  1033.4 4.0 fusion.2
  1037.4 0.0 all-reduce.5.cloned.1.call-update
  1037.4 188.5 %all-reduce.5.cloned.1.call-done = bf16[128,2560]{1,0:T(8,128)(2,1)} async-done(((bf16[128,2560]{1,0:T(8,128)(2,1)}), bf16[128,2560]{1,0:T(8,128)(2,1)}) %all-reduce.5.cloned.1.call-update) | async-done | bytes 655376 | tf_op jit(solution)/shard_map/psum | solution.py:38
  1226.0 1.1 fusion.46
  1227.1 0.7 copy.22
  (13 shorter events, 0.0 us)
Async XLA Ops:
  6.5 684.4 %copy-start = (bf16[1,2560,256]{2,1,0:T(8,128)(2,1)S(1)}, bf16[1,2560,256]{2,1,0:T(8,128)(2,1)}, u32[]{:S(2)}) copy-start(bf16[1,2560,256]{2,1,0:T(8,128)(2,1)} %param.25) | copy-start | bytes 3932164
  6.5 147.6 %all-gather.7.cloned.1.call-start = ((), (), s32[]{:S(2)}) async-start(), calls=%async_computation.2 | async-start | bytes 2703360 | tf_op jit(solution)/shard_map/all_gather | solution.py:18
  7.3 282.4 %all-gather.11.cloned.1.call-start = ((), (), s32[]{:S(2)}) async-start(), calls=%async_computation.4 | async-start | bytes 2703360 | tf_op jit(solution)/shard_map/all_gather | solution.py:29
  8.0 417.3 %all-gather.9.cloned.1.call-start = ((), (), s32[]{:S(2)}) async-start(), calls=%async_computation.3 | async-start | bytes 2703360 | tf_op jit(solution)/shard_map/all_gather | solution.py:23
  8.7 145.4 %copy-start.2 = (f32[2560]{0:T(1024)S(1)}, f32[2560]{0:T(1024)}, u32[]{:S(2)}) copy-start(f32[2560]{0:T(1024)} %param.15) | copy-start | bytes 30724
  8.8 613.7 %all-reduce.3.cloned.1.call-start = ((), (), s32[]{:S(2)}) async-start(), calls=%async_computation.5 | async-start | bytes 1310720 | tf_op jit(solution)/shard_map/psum | solution.py:38
  156.4 273.7 %copy-start.4 = (s32[128,1]{0,1:T(1,128)S(1)}, s32[128,1]{0,1:T(1,128)}, u32[]{:S(2)}) copy-start(s32[128,1]{0,1:T(1,128)} %param.26) | copy-start | bytes 1540
  430.1 193.8 %copy-start.3 = (f32[2560]{0:T(1024)S(1)}, f32[2560]{0:T(1024)}, u32[]{:S(2)}) copy-start(f32[2560]{0:T(1024)} %param.19) | copy-start | bytes 30724
  622.5 1.5 copy-start.1
  627.0 62.1 %all-to-all-start = ((bf16[32,8,2560]{2,1,0:T(8,128)(2,1)}), bf16[32,8,2560]{2,1,0:T(8,128)(2,1)S(1)}, u32[]{:S(2)}, u32[]{:S(2)}) async-start(bf16[32,8,2560]{2,1,0:T(8,128)(2,1)} %fusion), calls=%async_computation | async-start | bytes 2621440 | tf_op jit(solution)/shard_map/all_to_all | solution.py:83
  636.4 175.3 %all-gather.13.cloned.1.call-start = ((), (), s32[]{:S(2)}) async-start(), calls=%async_computation.6 | async-start | bytes 1351680 | tf_op jit(solution)/shard_map/all_gather | solution.py:18
  694.9 118.4 %all-to-all-start.1 = ((bf16[32,8,2560]{2,1,0:T(8,128)(2,1)}), bf16[32,8,2560]{2,1,0:T(8,128)(2,1)S(1)}, u32[]{:S(2)}, u32[]{:S(2)}) async-start(bf16[32,8,2560]{2,1,0:T(8,128)(2,1)} %fusion.1), calls=%async_computation.1 | async-start | bytes 2621440 | tf_op jit(solution)/shard_map/all_to_all | solution.py:99
  746.6 66.7 %copy-start.5 = (f32[128,1]{0,1:T(1,128)S(1)}, f32[128,1]{0,1:T(1,128)}, u32[]{:S(2)}) copy-start(f32[128,1]{0,1:T(1,128)} %param.27) | copy-start | bytes 1540
  746.6 175.8 %all-gather.15.cloned.1.call-start = ((), (), s32[]{:S(2)}) async-start(), calls=%async_computation.7 | async-start | bytes 1351680 | tf_op jit(solution)/shard_map/all_gather | solution.py:23
  747.2 286.2 %all-gather.17.cloned.1.call-start = ((), (), s32[]{:S(2)}) async-start(), calls=%async_computation.8 | async-start | bytes 1351680 | tf_op jit(solution)/shard_map/all_gather | solution.py:29
  747.9 478.0 %all-reduce.5.cloned.1.call-start = ((), (), s32[]{:S(2)}) async-start(), calls=%async_computation.9 | async-start | bytes 1310720 | tf_op jit(solution)/shard_map/psum | solution.py:38
Sparse Core Ops, SparseCore 0:
  11.6 142.4 all-gather.6
  158.4 131.2 all-gather.10
  294.0 131.2 all-gather.8
  430.3 192.1 all-reduce.2
  642.0 169.6 all-gather.12
  816.6 105.8 all-gather.14
  927.5 105.8 all-gather.16
  1037.6 188.3 all-reduce.4
where the time goes:
time: 1240 us; the launch traced here: 1230 us
  waiting for transfers between devices  1090 us (88%)
  starting transfers between devices  61.4 us (5%)
  blocking collectives  41.5 us (3%)
  matrix products  21.7 us (2%)
  between operations  13.7 us (1%)
    psum x2, waiting for transfers between devices, tensor_total(): lax.psum(partial_value.astype(jnp.bfloat16), 'tensor').astype(jnp.float32)  380 us
    all_gather x2, waiting for transfers between devices, ffn_partial(): lax.all_gather(down_rows, 'expert', axis=0, tiled=True)  244 us
    all_gather x2, waiting for transfers between devices, ffn_partial(): lax.all_gather(up_rows, 'expert', axis=0, tiled=True)  243 us
    all_gather x2, waiting for transfers between devices, ffn_partial(): lax.all_gather(gate_rows, 'expert', axis=0, tiled=True)  167 us
    all_to_all x1, waiting for transfers between devices, local(): lax.all_to_all(gathered.astype(jnp.bfloat16).reshape(experts, slot_depth,...  52.1 us
    all_to_all x1, starting transfers between devices, local(): lax.all_to_all(expert_out, 'expert', split_axis=0, concat_axis=0, tiled=T...  51.7 us
    all_gather x1, blocking collectives, local(): full_tokens = lax.all_gather(tokens, 'tensor', axis=1, tiled=True)  41.5 us
  transfers between devices with their start and end apart: 10, of which 9 were waited for; matrix products, arithmetic and copies ran while one was open for 1% of the time, Pallas kernels for 0%

commit v1 on v0

v1 whole, which is shorter than its diff:
```python
import jax
import jax.numpy as jnp
from jax import lax
from jax.experimental import pallas as pl
from jax.experimental.pallas import tpu as pltpu
from jax.sharding import PartitionSpec as P

EPSILON = 1e-05
MESH = pl.DeviceIdType.MESH
F32 = jnp.float32
BF16 = jnp.bfloat16

D = 2560
TOK = 128
FEAT = 160
ROWS = 80
HALF = D // 2
DEPTH = 8

NN = (((1,), (0,)), ((), ()))
NT = (((1,), (1,)), ((), ()))
TN = (((0,), (0,)), ((), ()))

PLANE = [(a, b) for a in range(4) for b in range(4) if (a, b) != (0, 0)]
PARTNERS = (
    [(a, b, 0, 0) for a, b in PLANE]
    + [(0, 0, d, 0) for d in (1, 2, 4, 8, 12, 14, 15)]
    + [(0, 0, 0, 1)]
)
NEAR = (1, 15, 2)
RING = (1, 3, 2)


def dot(a, b, dims):
    return lax.dot_general(a, b, dims, preferred_element_type=F32)


def identity(n):
    return (
        lax.broadcasted_iota(jnp.int32, (n, n), 0) == lax.broadcasted_iota(jnp.int32, (n, n), 1)
    ).astype(BF16)


def gated(gate_part, up_part):
    return (gate_part * jax.nn.sigmoid(gate_part) * up_part).astype(BF16)


N_SEM = 160


def kernel(
    tokens_ref, first_gain_ref, dense_gate_ref, dense_up_ref, dense_down_ref,
    second_gain_ref, shared_gate_ref, shared_up_ref, shared_down_ref,
    expert_gate_ref, expert_up_ref, expert_down_ref, routes_ref, route_gate_ref,
    out_ref,
    weights, staged, eg, eu, ed, ag0, ag1, xn, token_block, slot_matrix,
    routes_all, gates_all, part, sib0, sib1, sums0, sums1, near0, near1, mid0, mid1, far0, far1,
    accum, slots_out, slots_in, hidden_acc, expert_out, expert_sib, back_out, back_in, part1,
    send_sem, recv_sem, local_sem,
):
    e = lax.axis_index("expert")
    t = lax.axis_index("tensor")
    y, x, zh = e // 8, lax.rem(e // 2, 4), lax.rem(e, 2)
    z = zh * 8 + t // 2
    c = lax.rem(t, 2)
    zq, zr = z // 4, lax.rem(z, 4)
    other = 1 - zh
    oc = 1 - c

    def device(dy, dx, dz, dc):
        yy, xx = lax.rem(y + dy, 4), lax.rem(x + dx, 4)
        zz, cc = lax.rem(z + dz, 16), lax.rem(c + dc, 2)
        return {"expert": (yy * 4 + xx) * 2 + zz // 8, "tensor": lax.rem(zz, 8) * 2 + cc}

    counter = [0]
    pending = []

    def send(src, dst, offset):
        k = counter[0]
        counter[0] += 1
        copy = pltpu.make_async_remote_copy(
            src_ref=src,
            dst_ref=dst,
            send_sem=send_sem.at[k],
            recv_sem=recv_sem.at[k],
            device_id=device(*offset),
            device_id_type=MESH,
        )
        copy.start()
        pending.append(copy)
        return copy

    def landed(copies):
        for copy in copies:
            copy.wait_recv()

    loads = [
        pltpu.make_async_copy(src.at[0], dst, local_sem.at[i])
        for i, (src, dst) in enumerate(
            ((expert_gate_ref, eg), (expert_up_ref, eu), (expert_down_ref, ed))
        )
    ]
    for load in loads:
        load.start()

    barrier = pltpu.get_barrier_semaphore()
    for offset in PARTNERS:
        pl.semaphore_signal(barrier, inc=1, device_id=device(*offset), device_id_type=MESH)

    dense_refs = (dense_gate_ref, dense_up_ref, dense_down_ref)
    shared_refs = (shared_gate_ref, shared_up_ref, shared_down_ref)
    mine = pl.multiple_of(zh * 256, 256)
    theirs = pl.multiple_of(other * 256, 256)
    for i, ref in enumerate(dense_refs):
        for h in range(2):
            weights[3 * h + i, y, x, zh] = ref[:, pl.ds(mine + 128 * h, 128)]
            staged[3 * h + i] = ref[:, pl.ds(theirs + 128 * h, 128)]
    mine = pl.multiple_of(zh * 128, 128)
    theirs = pl.multiple_of(other * 128, 128)
    for i, ref in enumerate(shared_refs):
        weights[6 + i, y, x, zh] = ref[:, pl.ds(mine, 128)]
        staged[6 + i] = ref[:, pl.ds(theirs, 128)]
    tokens_t = dot(identity(FEAT), tokens_ref[...], NT).astype(BF16)
    token_block[...] = tokens_t
    ag0[zq, zr, c] = tokens_t

    routes_rows = jnp.broadcast_to(routes_ref[...].astype(F32), (TOK, TOK)).T
    gates_rows = jnp.broadcast_to(route_gate_ref[...], (TOK, TOK)).T
    routes_all[zh] = routes_rows[:8].astype(jnp.int32)
    gates_all[zh] = gates_rows[:8]

    pl.semaphore_wait(barrier, len(PARTNERS))

    def plane_first(unit, half, x_first):
        lo, n = unit
        block = weights.at[pl.ds(lo, n), y, x, half]
        return [
            send(block, block, (0, d, 0, 0) if x_first else (d, 0, 0, 0)) for d in RING
        ]

    def plane_second(unit, half, x_first):
        lo, n = unit
        if x_first:
            block = weights.at[pl.ds(lo, n), y, :, half]
            return [send(block, block, (d, 0, 0, 0)) for d in RING]
        block = weights.at[pl.ds(lo, n), :, x, half]
        return [send(block, block, (0, d, 0, 0)) for d in RING]

    A, B, S = (0, 3), (3, 3), (6, 3)

    def gather_far(buf):
        own = buf.at[zq, zr, c]
        return [send(own, own, (0, 0, d, 0)) for d in (8, 4, 12)]

    def gather_near(buf):
        block = buf.at[:, zr, c]
        return [send(block, block, (0, 0, d, 0)) for d in NEAR]

    def gather_sibling(buf):
        block = buf.at[:, :, c]
        return [send(block, block, (0, 0, 0, 1))]

    own_a = plane_first(A, zh, True)
    own_b = plane_first(B, zh, False)
    cross = [
        send(staged.at[pl.ds(lo, n)], weights.at[pl.ds(lo, n), y, x, zh], (0, 0, 8, 0))
        for lo, n in ((0, 6),)
    ]
    far = gather_far(ag0)
    cross_meta = [
        send(routes_all.at[zh], routes_all.at[zh], (0, 0, 8, 0)),
        send(gates_all.at[zh], gates_all.at[zh], (0, 0, 8, 0)),
    ]
    landed(own_a)
    own_a2 = plane_second(A, zh, True)
    landed(own_b)
    own_b2 = plane_second(B, zh, False)
    landed(cross)
    part_a = plane_first(A, other, True)
    part_b = plane_first(B, other, False)
    landed(far)
    near = gather_near(ag0)
    cross_s = [send(staged.at[pl.ds(6, 3)], weights.at[pl.ds(6, 3), y, x, zh], (0, 0, 8, 0))]
    landed(part_a)
    part_a2 = plane_second(A, other, True)
    landed(part_b)
    part_b2 = plane_second(B, other, False)
    own_s = plane_first(S, zh, True)

    landed(cross_meta)
    columns = []
    before = lax.broadcasted_iota(jnp.int32, (TOK, TOK), 0) < lax.broadcasted_iota(
        jnp.int32, (TOK, TOK), 1
    )
    for h in range(2):
        row = jnp.broadcast_to(routes_all[h][:1], (TOK, TOK))
        column = row.astype(F32).T.astype(jnp.int32)
        rank = jnp.sum(((row == column) & before).astype(F32), axis=0, keepdims=True)
        row = row[:1]
        slot = jnp.where((row & 1) == zh, (row >> 1) * 16 + h * DEPTH + rank.astype(jnp.int32), -1)
        columns.append(lax.broadcasted_iota(jnp.int32, (256, TOK), 0) == slot)
    slot_matrix[...] = jnp.concatenate(columns, axis=1).astype(F32).astype(BF16)

    def normalise(buf, gain_ref):
        eye = identity(TOK)
        squares = [jnp.zeros((TOK, 1), F32)] * 2
        for i in range(4):
            for h in range(2):
                block = buf[2 * h + i // 2, (2 * i) % 4 : (2 * i) % 4 + 2].reshape(640, TOK)
                rows = dot(eye, block, NT)
                xn[h * TOK : (h + 1) * TOK, 640 * i : 640 * (i + 1)] = rows.astype(BF16)
                squares[h] = squares[h] + jnp.sum(rows * rows, axis=1, keepdims=True)
        for h in range(2):
            scale = lax.rsqrt(squares[h] * (1.0 / D) + EPSILON)
            for i in range(4):
                at = (slice(h * TOK, (h + 1) * TOK), slice(640 * i, 640 * (i + 1)))
                gain = gain_ref[:, 640 * i : 640 * (i + 1)]
                xn[at] = (xn[at].astype(F32) * scale * gain).astype(BF16)

    landed(near)
    landed(gather_sibling(ag0))
    normalise(ag0, first_gain_ref)

    landed(own_a2 + own_b2 + part_a2 + part_b2)
    landed(cross_s)
    part_s = plane_first(S, other, False)

    def columns_of(blocks, yy):
        return jnp.concatenate([weights[b, yy].reshape(640, 128) for b in blocks], axis=1)

    hidden = jnp.zeros((256, 512), F32)
    for yy in range(4):
        hidden += dot(xn[:, 640 * yy : 640 * (yy + 1)], columns_of((0, 3, 1, 4), yy), NN)
    hidden = gated(hidden[:, :256], hidden[:, 256:])
    for zlo in range(8):
        rows = jnp.concatenate(
            [weights[b, zlo // 2, 2 * (zlo % 2) : 2 * (zlo % 2) + 2].reshape(320, 128) for b in (2, 5)],
            axis=1,
        )
        terms = dot(rows, hidden, NT).astype(BF16)
        for h in range(2):
            part[2 * h + zlo // 4, zlo % 4] = terms[:, h * TOK : (h + 1) * TOK].reshape(2, FEAT, TOK)

    landed(own_s)
    own_s2 = plane_second(S, zh, True)
    landed(part_s)
    part_s2 = plane_second(S, other, False)

    def reduce_scatter(part, sib, sums, near_in, mid, far_in):
        landed([send(part.at[:, :, oc], sib, (0, 0, 0, 1))])
        for q in range(4):
            for r in range(4):
                sums[q, r] = (part[q, r, c].astype(F32) + sib[q, r].astype(F32)).astype(BF16)
        landed(
            [
                send(sums.at[:, lax.rem(z + d, 4)], near_in.at[i], (0, 0, d, 0))
                for i, d in enumerate(NEAR)
            ]
        )
        for q in range(4):
            total = sums[q, zr].astype(F32)
            for i in range(3):
                total += near_in[i, q].astype(F32)
            mid[q] = total.astype(BF16)
        landed(
            [
                send(mid.at[lax.rem(zq + a, 4)], far_in.at[a - 1], (0, 0, 4 * a, 0))
                for a in (2, 1, 3)
            ]
        )
        total = mid[zq].astype(F32)
        for i in range(3):
            total += far_in[i].astype(F32)
        return total

    middle = token_block[...].astype(F32) + reduce_scatter(part, sib0, sums0, near0, mid0, far0)
    middle = middle.astype(BF16)
    token_block[...] = middle
    ag1[zq, zr, c] = middle
    landed(gather_far(ag1))
    landed(gather_near(ag1))
    landed(gather_sibling(ag1))
    normalise(ag1, second_gain_ref)

    half = pl.multiple_of(c * HALF, HALF)
    for i in range(5):
        piece = dot(slot_matrix[...], xn[:, pl.ds(half + 256 * i, 256)], NN)
        slots_out[:, 256 * i : 256 * (i + 1)] = piece.astype(BF16)

    def rows_of(yy, xx):
        return pl.ds(pl.multiple_of((yy * 4 + xx) * 16, 16), 16)

    own_rows = rows_of(y, x)

    def exchange(src, dst):
        return [
            send(
                src.at[rows_of(lax.rem(y + a, 4), lax.rem(x + b, 4))],
                dst.at[own_rows],
                (a, b, 0, 0),
            )
            for a, b in PLANE
        ]

    dispatched = exchange(slots_out, slots_in.at[c])
    slots_in[c, own_rows] = slots_out[own_rows]

    landed(own_s2 + part_s2)
    hidden = jnp.zeros((256, 256), F32)
    for yy in range(4):
        hidden += dot(xn[:, 640 * yy : 640 * (yy + 1)], columns_of((6, 7), yy), NN)
    hidden = gated(hidden[:, :128], hidden[:, 128:])
    for yy in range(4):
        accum[640 * yy : 640 * (yy + 1)] = dot(weights[8, yy].reshape(640, 128), hidden, NT)

    landed(dispatched)
    swapped = send(slots_in.at[c], slots_in.at[c], (0, 0, 0, 1))
    for load in loads:
        load.wait()

    def expert_half(h):
        base = pl.multiple_of(h * HALF, HALF)
        rows = slots_in.at[h]
        for i in range(5):
            k = pl.ds(base + 256 * i, 256)
            piece = rows[:, 256 * i : 256 * (i + 1)]
            hidden_acc[:, :256] += dot(piece, eg[k, :], NN)
            hidden_acc[:, 256:] += dot(piece, eu[k, :], NN)

    hidden_acc[...] = jnp.zeros_like(hidden_acc)
    expert_half(c)
    landed([swapped])
    expert_half(oc)
    hidden = gated(hidden_acc[:, :256], hidden_acc[:, 256:])
    for i in range(10):
        rows = dot(hidden, ed[256 * i : 256 * (i + 1), :], NT)
        expert_out[i // 5, :, 256 * (i % 5) : 256 * (i % 5 + 1)] = rows.astype(BF16)
    landed([send(expert_out.at[oc], expert_sib, (0, 0, 0, 1))])
    for i in range(5):
        at = (slice(None), slice(256 * i, 256 * (i + 1)))
        back_out[at] = (expert_out[c, :, 256 * i : 256 * (i + 1)].astype(F32) + expert_sib[at].astype(F32)).astype(BF16)
    returned = exchange(back_out, back_in)
    back_in[own_rows] = back_out[own_rows]
    landed(returned)

    gates = jnp.concatenate([gates_all[0][:1], gates_all[1][:1]], axis=1)
    for i in range(5):
        routed = dot(back_in[:, 256 * i : 256 * (i + 1)], slot_matrix[...], TN)
        accum[pl.ds(half + 256 * i, 256)] += routed * gates
    for zlo in range(8):
        terms = accum[320 * zlo : 320 * (zlo + 1)].astype(BF16)
        for h in range(2):
            part1[2 * h + zlo // 4, zlo % 4] = terms[:, h * TOK : (h + 1) * TOK].reshape(2, FEAT, TOK)
    mixed = token_block[...].astype(F32) + reduce_scatter(part1, sib1, sums1, near1, mid1, far1)
    out_ref[...] = dot(identity(TOK), mixed.astype(BF16), NT).astype(BF16)
    for copy in pending:
        copy.wait_send()


def local(*args):
    args = list(args)
    args[1] = args[1].reshape(1, D)
    args[5] = args[5].reshape(1, D)
    vmem = pl.BlockSpec(memory_space=pltpu.VMEM)
    anywhere = pl.BlockSpec(memory_space=pl.ANY)
    ring = (4, 4, FEAT, TOK)
    scratch = [
        ((9, 4, 4, 2, ROWS, 128), BF16),
        ((9, ROWS, 128), BF16),
        ((D, 256), BF16),
        ((D, 256), BF16),
        ((D, 256), BF16),
        ((4, 4, 2, FEAT, TOK), BF16),
        ((4, 4, 2, FEAT, TOK), BF16),
        ((256, D), BF16),
        ((FEAT, TOK), BF16),
        ((256, 256), BF16),
        ((2, 8, TOK), jnp.int32),
        ((2, 8, TOK), F32),
        ((4, 4, 2, FEAT, TOK), BF16),
        (ring, BF16),
        (ring, BF16),
        (ring, BF16),
        (ring, BF16),
        ((3, 4, FEAT, TOK), BF16),
        ((3, 4, FEAT, TOK), BF16),
        ((4, FEAT, TOK), BF16),
        ((4, FEAT, TOK), BF16),
        ((3, FEAT, TOK), BF16),
        ((3, FEAT, TOK), BF16),
        ((D, 256), F32),
        ((256, HALF), BF16),
        ((2, 256, HALF), BF16),
        ((256, 512), F32),
        ((2, 256, HALF), BF16),
        ((256, HALF), BF16),
        ((256, HALF), BF16),
        ((256, HALF), BF16),
        ((4, 4, 2, FEAT, TOK), BF16),
    ]
    return pl.pallas_call(
        kernel,
        out_shape=jax.ShapeDtypeStruct((TOK, FEAT), BF16),
        in_specs=[anywhere if 9 <= i < 12 else vmem for i in range(14)],
        out_specs=vmem,
        scratch_shapes=[pltpu.VMEM(shape, dtype) for shape, dtype in scratch]
        + [
            pltpu.SemaphoreType.DMA((N_SEM,)),
            pltpu.SemaphoreType.DMA((N_SEM,)),
            pltpu.SemaphoreType.DMA((3,)),
        ],
        compiler_params=pltpu.CompilerParams(
            collective_id=0, has_side_effects=True, vmem_limit_bytes=56 * 2**20
        ),
    )(*args)


def solution(mesh):
    placed = (
        P("expert", "tensor"),
        P(),
        P("expert", "tensor"),
        P("expert", "tensor"),
        P("expert", "tensor"),
        P(),
        P("expert", "tensor"),
        P("expert", "tensor"),
        P("expert", "tensor"),
        P("expert", None, "tensor"),
        P("expert", None, "tensor"),
        P("expert", None, "tensor"),
        P("expert", None),
        P("expert", None),
    )
    return jax.shard_map(
        local, mesh=mesh, in_specs=placed, out_specs=P("expert", "tensor"), check_vma=False
    )
```

time: 1240 us -> 181 us (0.15)
  waiting for transfers between devices: 1090 us -> 0 us
  Pallas kernels: 0 us -> 172 us
  starting transfers between devices: 61.4 us -> 0 us
  blocking collectives: 41.5 us -> 0 us
  matrix products: 21.7 us -> 0 us
  between operations: 13.7 us -> 0.01 us
    all_gather x6 -> x0, waiting for transfers between devices: 654 us -> none  [the longest x2 244 us: ffn_partial(): lax.all_gather(down_rows, 'expert', axis=0, tiled=True)]
    psum x2 -> x0, waiting for transfers between devices: 380 us -> none  [tensor_total(): lax.psum(partial_value.astype(jnp.bfloat16), 'tensor').astype(jnp.float32)]
    pallas_call x0 -> x1, Pallas kernels: none -> 172 us  [local(): pl.pallas_call(kernel, out_shape=jax.ShapeDtypeStruct((TOK, FEAT), BF16),...]
    all_to_all x2 -> x0, starting transfers between devices: 61.1 us -> none  [the longest x1 51.7 us: local(): lax.all_to_all(expert_out, 'expert', split_axis=0, concat_axis=0, tiled=T...]
    all_to_all x2 -> x0, waiting for transfers between devices: 52.1 us -> none  [the longest x1 52.1 us: local(): lax.all_to_all(gathered.astype(jnp.bfloat16).reshape(experts, slot_depth,...]
    all_gather x1 -> x0, blocking collectives: 41.5 us -> none  [local(): full_tokens = lax.all_gather(tokens, 'tensor', axis=1, tiled=True)]
    dot_general x8 -> x0, matrix products: 21.7 us -> none  [the longest x2 8.85 us: ffn_partial(): lax.dot_general(hidden, lax.all_gather(down_rows, 'expert', axis=0, tiled...]
  transfers between devices with their start and end apart: 10 -> 0, of which waited for: 9 -> 0; matrix products, arithmetic and copies ran while one was open for 1% -> 0% of each run, Pallas kernels for 0% -> 0%
where the time goes in v1:
time: 181 us
  Pallas kernels  172 us (95%)
  local copies, waits for them, and re-layouts  8.44 us (5%)
    pallas_call x1, Pallas kernels, local(): pl.pallas_call(kernel, out_shape=jax.ShapeDtypeStruct((TOK, FEAT), BF16),...  172 us
    unnamed x3, local copies, waits for them, and re-layouts  4.25 us

profile of v1, /device:TPU:1, one launch (start us, length us, event | category | flops | bytes accessed | tf_op | source)
XLA Modules:
  0.0 180.9 jit_solution(14435994968315599717)
XLA Ops:
  0.0 1.3 reshape.6.first_gain_ref
  1.3 1.3 reshape.7.second_gain_ref
  2.6 1.5 copy.15.tokens_ref
  4.1 1.4 copy.16.routes_ref
  5.5 1.4 copy.17.route_gate_ref
  6.9 172.5 %shard_map.136 = bf16[128,160]{1,0:T(8,128)(2,1)} custom-call(bf16[128,160]{1,0:T(8,128)(2,1)} %copy.15.tokens_ref, f32[1,2560]{1,0:T(1,128)} %reshape.6.first_gain_ref, bf16[80,512]{1,0:T(8,128)(2,1)} %dense_gate_ref.1, bf16[80,512]{1,0:T(8,128)(2,1)} %dense_up_ref.1, bf16[80,512]{1,0:T(8,128)(2,1)} %dense_down_ref.1, f32[1,2560]{1,0:T(1,128)} %reshape.7.second_gain_ref, ...), custom_call_target="tpu_custom_call" | custom-call | tf_op jit(solution)/shard_map/pallas_call | solution.py:401
  179.4 1.6 copy.18

commit v2 on v1

--- a/solution.py
+++ b/solution.py
@@ -24,10 +24,9 @@
 PLANE = [(a, b) for a in range(4) for b in range(4) if (a, b) != (0, 0)]
 PARTNERS = (
     [(a, b, 0, 0) for a, b in PLANE]
-    + [(0, 0, d, 0) for d in (1, 2, 4, 8, 12, 14, 15)]
+    + [(0, 0, d, 0) for d in (1, 2, 3, 8, 13, 14, 15)]
     + [(0, 0, 0, 1)]
 )
-NEAR = (1, 15, 2)
 RING = (1, 3, 2)
 
 
@@ -45,7 +44,7 @@
     return (gate_part * jax.nn.sigmoid(gate_part) * up_part).astype(BF16)
 
 
-N_SEM = 160
+N_SEM = 256
 
 
 def kernel(
@@ -54,7 +53,7 @@
     expert_gate_ref, expert_up_ref, expert_down_ref, routes_ref, route_gate_ref,
     out_ref,
     weights, staged, eg, eu, ed, ag0, ag1, xn, token_block, slot_matrix,
-    routes_all, gates_all, part, sib0, sib1, sums0, sums1, near0, near1, mid0, mid1, far0, far1,
+    routes_all, gates_all, part, sib0, sib1, sums0, sums1, came0, came1, six, passed0, passed1,
     accum, slots_out, slots_in, hidden_acc, expert_out, expert_sib, back_out, back_in, part1,
     send_sem, recv_sem, local_sem,
 ):
@@ -63,13 +62,13 @@
     y, x, zh = e // 8, lax.rem(e // 2, 4), lax.rem(e, 2)
     z = zh * 8 + t // 2
     c = lax.rem(t, 2)
-    zq, zr = z // 4, lax.rem(z, 4)
+    side = 1 - 2 * c
     other = 1 - zh
     oc = 1 - c
 
     def device(dy, dx, dz, dc):
         yy, xx = lax.rem(y + dy, 4), lax.rem(x + dx, 4)
-        zz, cc = lax.rem(z + dz, 16), lax.rem(c + dc, 2)
+        zz, cc = lax.rem(z + dz + 16, 16), lax.rem(c + dc, 2)
         return {"expert": (yy * 4 + xx) * 2 + zz // 8, "tensor": lax.rem(zz, 8) * 2 + cc}
 
     counter = [0]
@@ -120,14 +119,10 @@
     for i, ref in enumerate(shared_refs):
         weights[6 + i, y, x, zh] = ref[:, pl.ds(mine, 128)]
         staged[6 + i] = ref[:, pl.ds(theirs, 128)]
-    tokens_t = dot(identity(FEAT), tokens_ref[...], NT).astype(BF16)
-    token_block[...] = tokens_t
-    ag0[zq, zr, c] = tokens_t
-
-    routes_rows = jnp.broadcast_to(routes_ref[...].astype(F32), (TOK, TOK)).T
-    gates_rows = jnp.broadcast_to(route_gate_ref[...], (TOK, TOK)).T
-    routes_all[zh] = routes_rows[:8].astype(jnp.int32)
-    gates_all[zh] = gates_rows[:8]
+    ag0[z, c] = tokens_ref[...]
+
+    routes_all[zh] = jnp.broadcast_to(routes_ref[...], (8, TOK))
+    gates_all[zh] = jnp.broadcast_to(route_gate_ref[...], (8, TOK))
 
     pl.semaphore_wait(barrier, len(PARTNERS))
 
@@ -148,25 +143,50 @@
 
     A, B, S = (0, 3), (3, 3), (6, 3)
 
-    def gather_far(buf):
-        own = buf.at[zq, zr, c]
-        return [send(own, own, (0, 0, d, 0)) for d in (8, 4, 12)]
-
-    def gather_near(buf):
-        block = buf.at[:, zr, c]
-        return [send(block, block, (0, 0, d, 0)) for d in NEAR]
-
-    def gather_sibling(buf):
-        block = buf.at[:, :, c]
-        return [send(block, block, (0, 0, 0, 1))]
+    def spot(offset):
+        return lax.rem(z + offset + 16, 16)
+
+    def pass_on(buf, origin, steps):
+        block = buf.at[spot(origin), c]
+        return [send(block, block, (0, 0, step, 0)) for step in steps]
+
+    def gather_start(buf):
+        return pass_on(buf, 0, (3, -3, 1, -1)), pass_across(buf, (0,))
+
+    def pass_across(buf, origins):
+        blocks = [buf.at[spot(origin), c] for origin in origins]
+        return [send(block, block, (0, 0, 0, 1)) for block in blocks]
+
+    def gather_middle(buf, first, across):
+        landed(first[:1])
+        second = pass_on(buf, -3, (3, 1, -1))
+        landed(first[1:2])
+        second += pass_on(buf, 3, (-3, -1, 1))
+        landed(first[2:])
+        across += pass_across(buf, (-3, 3, -1, 1))
+        return second
+
+    def gather_end(buf, second, across):
+        landed(second[:1])
+        third = pass_on(buf, -6, (1, -1))
+        landed(second[3:4])
+        third += pass_on(buf, 6, (-1, 1))
+        third += pass_on(buf, -6 * side, (2 * side,))
+        landed(second[1:3] + second[4:])
+        across += pass_across(buf, (-6, 6, -4, -2, 4, 2))
+        landed(third)
+        across += pass_across(buf, (-7, -5, 7, 5, 8))
+        landed(across)
 
     own_a = plane_first(A, zh, True)
     own_b = plane_first(B, zh, False)
-    cross = [
-        send(staged.at[pl.ds(lo, n)], weights.at[pl.ds(lo, n), y, x, zh], (0, 0, 8, 0))
-        for lo, n in ((0, 6),)
-    ]
-    far = gather_far(ag0)
+    def cross_over(lo, n):
+        block = weights.at[pl.ds(lo, n), y, x, zh]
+        return [send(staged.at[pl.ds(lo, n)], block, (0, 0, 8, 0))]
+
+    order = (0, 1, 3, 4, 2, 5)
+    cross = [cross_over(b, 1) for b in order]
+    first, across = gather_start(ag0)
     cross_meta = [
         send(routes_all.at[zh], routes_all.at[zh], (0, 0, 8, 0)),
         send(gates_all.at[zh], gates_all.at[zh], (0, 0, 8, 0)),
@@ -175,17 +195,32 @@
     own_a2 = plane_second(A, zh, True)
     landed(own_b)
     own_b2 = plane_second(B, zh, False)
-    landed(cross)
-    part_a = plane_first(A, other, True)
-    part_b = plane_first(B, other, False)
-    landed(far)
-    near = gather_near(ag0)
-    cross_s = [send(staged.at[pl.ds(6, 3)], weights.at[pl.ds(6, 3), y, x, zh], (0, 0, 8, 0))]
-    landed(part_a)
-    part_a2 = plane_second(A, other, True)
-    landed(part_b)
-    part_b2 = plane_second(B, other, False)
+    second = gather_middle(ag0, first, across)
+    part_1, part_2 = {}, {}
+
+    def crossed(i):
+        landed(cross[i])
+        part_1[i] = plane_first((order[i], 1), other, i % 2 == 0)
+
+    def spread(i):
+        landed(part_1[i])
+        part_2[i] = plane_second((order[i], 1), other, i % 2 == 0)
+
+    crossed(0)
+    crossed(1)
+    crossed(2)
+    spread(0)
+    crossed(3)
+    spread(1)
+    crossed(4)
+    spread(2)
+    crossed(5)
+    spread(3)
+    spread(4)
+    spread(5)
+    cross_s = cross_over(6, 3)
     own_s = plane_first(S, zh, True)
+    gather_end(ag0, second, across)
 
     landed(cross_meta)
     columns = []
@@ -206,7 +241,7 @@
         squares = [jnp.zeros((TOK, 1), F32)] * 2
         for i in range(4):
             for h in range(2):
-                block = buf[2 * h + i // 2, (2 * i) % 4 : (2 * i) % 4 + 2].reshape(640, TOK)
+                block = buf[8 * h + 2 * i : 8 * h + 2 * i + 2].reshape(640, TOK)
                 rows = dot(eye, block, NT)
                 xn[h * TOK : (h + 1) * TOK, 640 * i : 640 * (i + 1)] = rows.astype(BF16)
                 squares[h] = squares[h] + jnp.sum(rows * rows, axis=1, keepdims=True)
@@ -214,16 +249,13 @@
             scale = lax.rsqrt(squares[h] * (1.0 / D) + EPSILON)
             for i in range(4):
                 at = (slice(h * TOK, (h + 1) * TOK), slice(640 * i, 640 * (i + 1)))
-                gain = gain_ref[:, 640 * i : 640 * (i + 1)]
+                gain = gain_ref[640 * i : 640 * (i + 1)][None, :]
                 xn[at] = (xn[at].astype(F32) * scale * gain).astype(BF16)
 
-    landed(near)
-    landed(gather_sibling(ag0))
     normalise(ag0, first_gain_ref)
 
-    landed(own_a2 + own_b2 + part_a2 + part_b2)
-    landed(cross_s)
-    part_s = plane_first(S, other, False)
+    landed(own_a2 + own_b2)
+    landed(part_2[0] + part_2[1] + part_2[2] + part_2[3])
 
     def columns_of(blocks, yy):
         return jnp.concatenate([weights[b, yy].reshape(640, 128) for b in blocks], axis=1)
@@ -232,6 +264,7 @@
     for yy in range(4):
         hidden += dot(xn[:, 640 * yy : 640 * (yy + 1)], columns_of((0, 3, 1, 4), yy), NN)
     hidden = gated(hidden[:, :256], hidden[:, 256:])
+    landed(part_2[4] + part_2[5])
     for zlo in range(8):
         rows = jnp.concatenate(
             [weights[b, zlo // 2, 2 * (zlo % 2) : 2 * (zlo % 2) + 2].reshape(320, 128) for b in (2, 5)],
@@ -239,47 +272,78 @@
         )
         terms = dot(rows, hidden, NT).astype(BF16)
         for h in range(2):
-            part[2 * h + zlo // 4, zlo % 4] = terms[:, h * TOK : (h + 1) * TOK].reshape(2, FEAT, TOK)
-
-    landed(own_s)
-    own_s2 = plane_second(S, zh, True)
-    landed(part_s)
+            part[8 * h + zlo] = terms[:, h * TOK : (h + 1) * TOK].reshape(2, FEAT, TOK)
+
+    def reduce_scatter(part, sib, sums, came, six, passed, meanwhile):
+        deep = (-7, -5, 7, 5, 8)
+        middle = (-4, -2, 4, 2)
+        rest = (-6, 6, -3, 3, -1, 1, 0)
+        across = {
+            o: send(part.at[spot(o), oc], sib.at[spot(o)], (0, 0, 0, 1)) for o in deep + middle + rest
+        }
+
+        def add_cores(o):
+            landed([across[o]])
+            i = spot(o)
+            sums[i] = (part[i, c].astype(F32) + sib[i].astype(F32)).astype(BF16)
+
+        slots = [0]
+
+        def leave(o, step):
+            slots[0] += 1
+            slot = came.at[slots[0] - 1]
+            return slots[0] - 1, send(sums.at[spot(o)], slot, (0, 0, step, 0))
+
+        def arrived(*legs):
+            landed([leg[1] for leg in legs])
+            return sum(came[leg[0]].astype(F32) for leg in legs)
+
+        legs = {}
+        for o, step in zip(deep, (-1, 1, 1, -1, -2 * side)):
+            add_cores(o)
+            legs[o] = leave(o, step)
+        for o, step in zip(middle, (-1, 1, 1, -1)):
+            add_cores(o)
+            legs[o] = leave(o, step)
+        for o in rest:
+            add_cores(o)
+            if o in (-1, 1):
+                legs[o] = leave(o, o)
+        meanwhile()
+        six[0] = sums[spot(-6)].astype(F32) + arrived(legs[-7], legs[-5])
+        six[1] = sums[spot(6)].astype(F32) + arrived(legs[7], legs[5])
+        six[c] += arrived(legs[8])
+        for i, o in enumerate((-6, 6)):
+            passed[i] = six[i].astype(BF16)
+            slots[0] += 1
+            slot = came.at[slots[0] - 1]
+            legs[o] = (slots[0] - 1, send(passed.at[i], slot, (0, 0, -3 if o < 0 else 3, 0)))
+        for i, s in enumerate((-1, 1)):
+            three = sums[spot(3 * s)].astype(F32) + arrived(legs[2 * s], legs[4 * s]) + arrived(legs[6 * s])
+            passed[2 + i] = three.astype(BF16)
+            slots[0] += 1
+            slot = came.at[slots[0] - 1]
+            legs[3 * s] = (slots[0] - 1, send(passed.at[2 + i], slot, (0, 0, 3 * s, 0)))
+        total = sums[z].astype(F32) + arrived(legs[-1], legs[1])
+        return total + arrived(legs[-3], legs[3])
+
+    late = {}
+
+    def shared_weights():
+        landed(cross_s)
+        late["part"] = plane_first(S, other, False)
+        landed(own_s)
+        late["own"] = plane_second(S, zh, True)
+
+    middle = reduce_scatter(part, sib0, sums0, came0, six, passed0, shared_weights)
+    middle = (tokens_ref[...].astype(F32) + middle).astype(BF16)
+    token_block[...] = middle
+    ag1[z, c] = middle
+    first, across = gather_start(ag1)
+    landed(late["part"])
     part_s2 = plane_second(S, other, False)
-
-    def reduce_scatter(part, sib, sums, near_in, mid, far_in):
-        landed([send(part.at[:, :, oc], sib, (0, 0, 0, 1))])
-        for q in range(4):
-            for r in range(4):
-                sums[q, r] = (part[q, r, c].astype(F32) + sib[q, r].astype(F32)).astype(BF16)
-        landed(
-            [
-                send(sums.at[:, lax.rem(z + d, 4)], near_in.at[i], (0, 0, d, 0))
-                for i, d in enumerate(NEAR)
-            ]
-        )
-        for q in range(4):
-            total = sums[q, zr].astype(F32)
-            for i in range(3):
-                total += near_in[i, q].astype(F32)
-            mid[q] = total.astype(BF16)
-        landed(
-            [
-                send(mid.at[lax.rem(zq + a, 4)], far_in.at[a - 1], (0, 0, 4 * a, 0))
-                for a in (2, 1, 3)
-            ]
-        )
-        total = mid[zq].astype(F32)
-        for i in range(3):
-            total += far_in[i].astype(F32)
-        return total
-
-    middle = token_block[...].astype(F32) + reduce_scatter(part, sib0, sums0, near0, mid0, far0)
-    middle = middle.astype(BF16)
-    token_block[...] = middle
-    ag1[zq, zr, c] = middle
-    landed(gather_far(ag1))
-    landed(gather_near(ag1))
-    landed(gather_sibling(ag1))
+    second = gather_middle(ag1, first, across)
+    gather_end(ag1, second, across)
     normalise(ag1, second_gain_ref)
 
     half = pl.multiple_of(c * HALF, HALF)
@@ -305,7 +369,7 @@
     dispatched = exchange(slots_out, slots_in.at[c])
     slots_in[c, own_rows] = slots_out[own_rows]
 
-    landed(own_s2 + part_s2)
+    landed(late["own"] + part_s2)
     hidden = jnp.zeros((256, 256), F32)
     for yy in range(4):
         hidden += dot(xn[:, 640 * yy : 640 * (yy + 1)], columns_of((6, 7), yy), NN)
@@ -350,44 +414,45 @@
     for zlo in range(8):
         terms = accum[320 * zlo : 320 * (zlo + 1)].astype(BF16)
         for h in range(2):
-            part1[2 * h + zlo // 4, zlo % 4] = terms[:, h * TOK : (h + 1) * TOK].reshape(2, FEAT, TOK)
-    mixed = token_block[...].astype(F32) + reduce_scatter(part1, sib1, sums1, near1, mid1, far1)
-    out_ref[...] = dot(identity(TOK), mixed.astype(BF16), NT).astype(BF16)
+            part1[8 * h + zlo] = terms[:, h * TOK : (h + 1) * TOK].reshape(2, FEAT, TOK)
+    mixed = reduce_scatter(part1, sib1, sums1, came1, six, passed1, lambda: None)
+    mixed = token_block[...].astype(F32) + mixed
+    out_ref[...] = mixed.astype(BF16)
     for copy in pending:
         copy.wait_send()
 
 
 def local(*args):
     args = list(args)
-    args[1] = args[1].reshape(1, D)
-    args[5] = args[5].reshape(1, D)
+    args[0] = args[0].T
+    args[12] = args[12].reshape(1, TOK)
+    args[13] = args[13].reshape(1, TOK)
     vmem = pl.BlockSpec(memory_space=pltpu.VMEM)
     anywhere = pl.BlockSpec(memory_space=pl.ANY)
-    ring = (4, 4, FEAT, TOK)
+    ring = (16, FEAT, TOK)
     scratch = [
         ((9, 4, 4, 2, ROWS, 128), BF16),
         ((9, ROWS, 128), BF16),
         ((D, 256), BF16),
         ((D, 256), BF16),
         ((D, 256), BF16),
-        ((4, 4, 2, FEAT, TOK), BF16),
-        ((4, 4, 2, FEAT, TOK), BF16),
+        ((16, 2, FEAT, TOK), BF16),
+        ((16, 2, FEAT, TOK), BF16),
         ((256, D), BF16),
         ((FEAT, TOK), BF16),
         ((256, 256), BF16),
         ((2, 8, TOK), jnp.int32),
         ((2, 8, TOK), F32),
-        ((4, 4, 2, FEAT, TOK), BF16),
+        ((16, 2, FEAT, TOK), BF16),
         (ring, BF16),
         (ring, BF16),
         (ring, BF16),
         (ring, BF16),
-        ((3, 4, FEAT, TOK), BF16),
-        ((3, 4, FEAT, TOK), BF16),
+        ((15, FEAT, TOK), BF16),
+        ((15, FEAT, TOK), BF16),
+        ((2, FEAT, TOK), F32),
         ((4, FEAT, TOK), BF16),
         ((4, FEAT, TOK), BF16),
-        ((3, FEAT, TOK), BF16),
-        ((3, FEAT, TOK), BF16),
         ((D, 256), F32),
         ((256, HALF), BF16),
         ((2, 256, HALF), BF16),
@@ -396,11 +461,11 @@
         ((256, HALF), BF16),
         ((256, HALF), BF16),
         ((256, HALF), BF16),
-        ((4, 4, 2, FEAT, TOK), BF16),
+        ((16, 2, FEAT, TOK), BF16),
     ]
     return pl.pallas_call(
         kernel,
-        out_shape=jax.ShapeDtypeStruct((TOK, FEAT), BF16),
+        out_shape=jax.ShapeDtypeStruct((FEAT, TOK), BF16),
         in_specs=[anywhere if 9 <= i < 12 else vmem for i in range(14)],
         out_specs=vmem,
         scratch_shapes=[pltpu.VMEM(shape, dtype) for shape, dtype in scratch]
@@ -412,7 +477,7 @@
         compiler_params=pltpu.CompilerParams(
             collective_id=0, has_side_effects=True, vmem_limit_bytes=56 * 2**20
         ),
-    )(*args)
+    )(*args).T
 
 
 def solution(mesh):

time: 181 us -> 151 us (0.83)
  Pallas kernels: 172 us -> 149 us
  local copies, waits for them, and re-layouts: 8.44 us -> 1.4 us
    pallas_call x1, Pallas kernels: 172 us -> 149 us  [local(): pl.pallas_call(kernel, out_shape=jax.ShapeDtypeStruct((FEAT, TOK), BF16),...]
    unnamed x3 -> x1, local copies, waits for them, and re-layouts: 4.25 us -> 1.4 us
    reshape x2 -> x0, local copies, waits for them, and re-layouts: 2.62 us -> none  [the longest x1 1.31 us: local(): args[1] = args[1].reshape(1, D)]
where the time goes in v2:
time: 151 us
  Pallas kernels  149 us (99%)
    pallas_call x1, Pallas kernels, local(): pl.pallas_call(kernel, out_shape=jax.ShapeDtypeStruct((FEAT, TOK), BF16),...  149 us

profile of v2, /device:TPU:1, one launch (start us, length us, event | category | flops | bytes accessed | tf_op | source)
XLA Modules:
  0.0 150.5 jit_solution(11095108232889030977)
XLA Ops:
  0.0 149.1 %shard_map.136 = bf16[160,128]{1,0:T(8,128)(2,1)} custom-call(bf16[160,128]{1,0:T(8,128)(2,1)} %bitcast.5, f32[2560]{0:T(1024)} %first_gain_ref.1, bf16[80,512]{1,0:T(8,128)(2,1)} %dense_gate_ref.1, bf16[80,512]{1,0:T(8,128)(2,1)} %dense_up_ref.1, bf16[80,512]{1,0:T(8,128)(2,1)} %dense_down_ref.1, f32[2560]{0:T(1024)} %second_gain_ref.1, ...), custom_call_target="tpu_custom_call" | custom-call | tf_op jit(solution)/shard_map/pallas_call | solution.py:466
  149.1 1.4 copy.16

commit v3 on v2

--- a/solution.py
+++ b/solution.py
@@ -21,7 +21,10 @@
 NT = (((1,), (1,)), ((), ()))
 TN = (((0,), (0,)), ((), ()))
 
-PLANE = [(a, b) for a in range(4) for b in range(4) if (a, b) != (0, 0)]
+PLANE = sorted(
+    [(a, b) for a in range(4) for b in range(4) if (a, b) != (0, 0)],
+    key=lambda place: -min(place[0], 4 - place[0]) - min(place[1], 4 - place[1]),
+)
 PARTNERS = (
     [(a, b, 0, 0) for a, b in PLANE]
     + [(0, 0, d, 0) for d in (1, 2, 3, 8, 13, 14, 15)]
@@ -44,7 +47,7 @@
     return (gate_part * jax.nn.sigmoid(gate_part) * up_part).astype(BF16)
 
 
-N_SEM = 256
+N_SEM = 320
 
 
 def kernel(
@@ -166,7 +169,7 @@
         across += pass_across(buf, (-3, 3, -1, 1))
         return second
 
-    def gather_end(buf, second, across):
+    def gather_late(buf, second, across):
         landed(second[:1])
         third = pass_on(buf, -6, (1, -1))
         landed(second[3:4])
@@ -174,53 +177,86 @@
         third += pass_on(buf, -6 * side, (2 * side,))
         landed(second[1:3] + second[4:])
         across += pass_across(buf, (-6, 6, -4, -2, 4, 2))
+        return third
+
+    def gather_end(buf, third, across):
         landed(third)
         across += pass_across(buf, (-7, -5, 7, 5, 8))
         landed(across)
 
-    own_a = plane_first(A, zh, True)
-    own_b = plane_first(B, zh, False)
+    def plane_beside(unit, half, x_first):
+        lo, n = unit
+        if x_first:
+            block = weights.at[pl.ds(lo, n), y, :, half]
+            return [send(block, block, (d, 0, 0, 0)) for d in (1, 3)]
+        block = weights.at[pl.ds(lo, n), :, x, half]
+        return [send(block, block, (0, d, 0, 0)) for d in (1, 3)]
+
+    def plane_beyond(unit, half, x_first, beside):
+        lo, n = unit
+        passed_on = []
+        for copy, d, rows in zip(beside, (1, 3), (slice(0, 2), slice(2, 4))):
+            landed([copy])
+            if x_first:
+                block = weights.at[pl.ds(lo, n), lax.rem(y + 4 - d, 4), rows, half]
+                passed_on.append(send(block, block, (d, 0, 0, 0)))
+            else:
+                block = weights.at[pl.ds(lo, n), rows, lax.rem(x + 4 - d, 4), half]
+                passed_on.append(send(block, block, (0, d, 0, 0)))
+        return passed_on
+
     def cross_over(lo, n):
         block = weights.at[pl.ds(lo, n), y, x, zh]
         return [send(staged.at[pl.ds(lo, n)], block, (0, 0, 8, 0))]
 
+    first, across = gather_start(ag0)
+    own_a = plane_first(A, zh, True)
+    own_b = plane_first(B, zh, False)
     order = (0, 1, 3, 4, 2, 5)
     cross = [cross_over(b, 1) for b in order]
-    first, across = gather_start(ag0)
     cross_meta = [
         send(routes_all.at[zh], routes_all.at[zh], (0, 0, 8, 0)),
         send(gates_all.at[zh], gates_all.at[zh], (0, 0, 8, 0)),
     ]
-    landed(own_a)
-    own_a2 = plane_second(A, zh, True)
-    landed(own_b)
-    own_b2 = plane_second(B, zh, False)
-    second = gather_middle(ag0, first, across)
-    part_1, part_2 = {}, {}
+    part_1, part_2, part_3 = {}, {}, {}
 
     def crossed(i):
         landed(cross[i])
         part_1[i] = plane_first((order[i], 1), other, i % 2 == 0)
 
-    def spread(i):
+    def beside(i):
         landed(part_1[i])
-        part_2[i] = plane_second((order[i], 1), other, i % 2 == 0)
-
+        part_2[i] = plane_beside((order[i], 1), other, i % 2 == 0)
+
+    def beyond(i):
+        part_3[i] = plane_beyond((order[i], 1), other, i % 2 == 0, part_2[i])
+
+    landed(own_a)
+    own_a2 = plane_beside(A, zh, True)
+    landed(own_b)
+    own_b2 = plane_beside(B, zh, False)
+    second = gather_middle(ag0, first, across)
     crossed(0)
     crossed(1)
     crossed(2)
-    spread(0)
+    beside(0)
     crossed(3)
-    spread(1)
+    beside(1)
     crossed(4)
-    spread(2)
+    own_3 = plane_beyond(A, zh, True, own_a2) + plane_beyond(B, zh, False, own_b2)
+    third = gather_late(ag0, second, across)
+    cross_s = cross_over(6, 3)
+    beside(2)
     crossed(5)
-    spread(3)
-    spread(4)
-    spread(5)
-    cross_s = cross_over(6, 3)
+    beside(3)
+    beyond(0)
+    beside(4)
+    beyond(1)
+    beside(5)
+    for i in range(2, 6):
+        beyond(i)
     own_s = plane_first(S, zh, True)
-    gather_end(ag0, second, across)
+    gather_end(ag0, third, across)
 
     landed(cross_meta)
     columns = []
@@ -254,8 +290,7 @@
 
     normalise(ag0, first_gain_ref)
 
-    landed(own_a2 + own_b2)
-    landed(part_2[0] + part_2[1] + part_2[2] + part_2[3])
+    landed(own_3 + part_3[0] + part_3[1] + part_3[2] + part_3[3])
 
     def columns_of(blocks, yy):
         return jnp.concatenate([weights[b, yy].reshape(640, 128) for b in blocks], axis=1)
@@ -264,7 +299,7 @@
     for yy in range(4):
         hidden += dot(xn[:, 640 * yy : 640 * (yy + 1)], columns_of((0, 3, 1, 4), yy), NN)
     hidden = gated(hidden[:, :256], hidden[:, 256:])
-    landed(part_2[4] + part_2[5])
+    landed(part_3[4] + part_3[5])
     for zlo in range(8):
         rows = jnp.concatenate(
             [weights[b, zlo // 2, 2 * (zlo % 2) : 2 * (zlo % 2) + 2].reshape(320, 128) for b in (2, 5)],
@@ -309,7 +344,6 @@
             add_cores(o)
             if o in (-1, 1):
                 legs[o] = leave(o, o)
-        meanwhile()
         six[0] = sums[spot(-6)].astype(F32) + arrived(legs[-7], legs[-5])
         six[1] = sums[spot(6)].astype(F32) + arrived(legs[7], legs[5])
         six[c] += arrived(legs[8])
@@ -318,6 +352,7 @@
             slots[0] += 1
             slot = came.at[slots[0] - 1]
             legs[o] = (slots[0] - 1, send(passed.at[i], slot, (0, 0, -3 if o < 0 else 3, 0)))
+        meanwhile()
         for i, s in enumerate((-1, 1)):
             three = sums[spot(3 * s)].astype(F32) + arrived(legs[2 * s], legs[4 * s]) + arrived(legs[6 * s])
             passed[2 + i] = three.astype(BF16)
@@ -343,7 +378,8 @@
     landed(late["part"])
     part_s2 = plane_second(S, other, False)
     second = gather_middle(ag1, first, across)
-    gather_end(ag1, second, across)
+    third = gather_late(ag1, second, across)
+    gather_end(ag1, third, across)
     normalise(ag1, second_gain_ref)
 
     half = pl.multiple_of(c * HALF, HALF)
@@ -377,8 +413,12 @@
     for yy in range(4):
         accum[640 * yy : 640 * (yy + 1)] = dot(weights[8, yy].reshape(640, 128), hidden, NT)
 
-    landed(dispatched)
-    swapped = send(slots_in.at[c], slots_in.at[c], (0, 0, 0, 1))
+    swapped = []
+    for k, (a, b) in enumerate([(0, 0)] + PLANE):
+        if k:
+            landed(dispatched[k - 1 : k])
+        block = slots_in.at[c, rows_of(lax.rem(y + 4 - a, 4), lax.rem(x + 4 - b, 4))]
+        swapped.append(send(block, block, (0, 0, 0, 1)))
     for load in loads:
         load.wait()
 
@@ -393,16 +433,23 @@
 
     hidden_acc[...] = jnp.zeros_like(hidden_acc)
     expert_half(c)
-    landed([swapped])
+    landed(swapped)
     expert_half(oc)
     hidden = gated(hidden_acc[:, :256], hidden_acc[:, 256:])
-    for i in range(10):
-        rows = dot(hidden, ed[256 * i : 256 * (i + 1), :], NT)
-        expert_out[i // 5, :, 256 * (i % 5) : 256 * (i % 5 + 1)] = rows.astype(BF16)
-    landed([send(expert_out.at[oc], expert_sib, (0, 0, 0, 1))])
+    def expert_rows(h, i):
+        k = pl.ds(pl.multiple_of(h * HALF, HALF) + 256 * i, 256)
+        return dot(hidden, ed[k, :], NT)
+
+    crossing = []
     for i in range(5):
-        at = (slice(None), slice(256 * i, 256 * (i + 1)))
-        back_out[at] = (expert_out[c, :, 256 * i : 256 * (i + 1)].astype(F32) + expert_sib[at].astype(F32)).astype(BF16)
+        cols = slice(256 * i, 256 * (i + 1))
+        expert_out[:, cols] = expert_rows(oc, i).astype(BF16)
+        crossing.append(send(expert_out.at[:, cols], expert_sib.at[:, cols], (0, 0, 0, 1)))
+    for i in range(5):
+        cols = slice(256 * i, 256 * (i + 1))
+        rows = expert_rows(c, i)
+        landed(crossing[i : i + 1])
+        back_out[:, cols] = (rows + expert_sib[:, cols].astype(F32)).astype(BF16)
     returned = exchange(back_out, back_in)
     back_in[own_rows] = back_out[own_rows]
     landed(returned)
@@ -418,6 +465,7 @@
     mixed = reduce_scatter(part1, sib1, sums1, came1, six, passed1, lambda: None)
     mixed = token_block[...].astype(F32) + mixed
     out_ref[...] = mixed.astype(BF16)
+    assert counter[0] <= N_SEM
     for copy in pending:
         copy.wait_send()
 
@@ -457,7 +505,7 @@
         ((256, HALF), BF16),
         ((2, 256, HALF), BF16),
         ((256, 512), F32),
-        ((2, 256, HALF), BF16),
+        ((256, HALF), BF16),
         ((256, HALF), BF16),
         ((256, HALF), BF16),
         ((256, HALF), BF16),

time: 151 us -> 142 us (0.940)
  Pallas kernels: 149 us -> 140 us
    pallas_call x1, Pallas kernels: 149 us -> 140 us  [local(): pl.pallas_call(kernel, out_shape=jax.ShapeDtypeStruct((FEAT, TOK), BF16),...]
where the time goes in v3:
time: 142 us; the launch traced here: 141 us
  Pallas kernels  140 us (99%)
    pallas_call x1, Pallas kernels, local(): pl.pallas_call(kernel, out_shape=jax.ShapeDtypeStruct((FEAT, TOK), BF16),...  140 us

profile of v3, /device:TPU:1, one launch (start us, length us, event | category | flops | bytes accessed | tf_op | source)
XLA Modules:
  0.0 141.3 jit_solution(4782145265104988886)
XLA Ops:
  0.0 139.9 %shard_map.136 = bf16[160,128]{1,0:T(8,128)(2,1)} custom-call(bf16[160,128]{1,0:T(8,128)(2,1)} %bitcast.5, f32[2560]{0:T(1024)} %first_gain_ref.1, bf16[80,512]{1,0:T(8,128)(2,1)} %dense_gate_ref.1, bf16[80,512]{1,0:T(8,128)(2,1)} %dense_up_ref.1, bf16[80,512]{1,0:T(8,128)(2,1)} %dense_down_ref.1, f32[2560]{0:T(1024)} %second_gain_ref.1, ...), custom_call_target="tpu_custom_call" | custom-call | tf_op jit(solution)/shard_map/pallas_call | solution.py:514
  139.9 1.4 copy.16

commit v4 on v3

--- a/solution.py
+++ b/solution.py
@@ -31,6 +31,7 @@
     + [(0, 0, 0, 1)]
 )
 RING = (1, 3, 2)
+HALVES = (slice(0, 80), slice(80, 160))
 
 
 def dot(a, b, dims):
@@ -149,33 +150,39 @@
     def spot(offset):
         return lax.rem(z + offset + 16, 16)
 
-    def pass_on(buf, origin, steps):
-        block = buf.at[spot(origin), c]
+    def pass_on(buf, origin, steps, rows=slice(0, FEAT)):
+        block = buf.at[spot(origin), c, rows]
         return [send(block, block, (0, 0, step, 0)) for step in steps]
-
-    def gather_start(buf):
-        return pass_on(buf, 0, (3, -3, 1, -1)), pass_across(buf, (0,))
 
     def pass_across(buf, origins):
         blocks = [buf.at[spot(origin), c] for origin in origins]
         return [send(block, block, (0, 0, 0, 1)) for block in blocks]
 
+    def gather_start(buf):
+        first = [pass_on(buf, 0, (3, -3), rows) for rows in HALVES]
+        return first + [pass_on(buf, 0, (1, -1))], pass_across(buf, (0,))
+
     def gather_middle(buf, first, across):
-        landed(first[:1])
-        second = pass_on(buf, -3, (3, 1, -1))
-        landed(first[1:2])
-        second += pass_on(buf, 3, (-3, -1, 1))
-        landed(first[2:])
+        second = []
+        for i, rows in enumerate(HALVES):
+            landed(first[i][:1])
+            forth = pass_on(buf, -3, (3,), rows)
+            landed(first[i][1:])
+            second.append(forth + pass_on(buf, 3, (-3,), rows))
+        second.append(pass_on(buf, -3, (1, -1)) + pass_on(buf, 3, (-1, 1)))
+        landed(first[2])
         across += pass_across(buf, (-3, 3, -1, 1))
         return second
 
     def gather_late(buf, second, across):
-        landed(second[:1])
-        third = pass_on(buf, -6, (1, -1))
-        landed(second[3:4])
-        third += pass_on(buf, 6, (-1, 1))
-        third += pass_on(buf, -6 * side, (2 * side,))
-        landed(second[1:3] + second[4:])
+        third = []
+        for i, rows in enumerate(HALVES):
+            landed(second[i][:1])
+            third += pass_on(buf, -6, (1, -1), rows)
+            landed(second[i][1:])
+            third += pass_on(buf, 6, (-1, 1), rows)
+            third += pass_on(buf, -6 * side, (2 * side,), rows)
+        landed(second[2])
         across += pass_across(buf, (-6, 6, -4, -2, 4, 2))
         return third
 
@@ -329,10 +336,6 @@
             slot = came.at[slots[0] - 1]
             return slots[0] - 1, send(sums.at[spot(o)], slot, (0, 0, step, 0))
 
-        def arrived(*legs):
-            landed([leg[1] for leg in legs])
-            return sum(came[leg[0]].astype(F32) for leg in legs)
-
         legs = {}
         for o, step in zip(deep, (-1, 1, 1, -1, -2 * side)):
             add_cores(o)
@@ -344,23 +347,34 @@
             add_cores(o)
             if o in (-1, 1):
                 legs[o] = leave(o, o)
-        six[0] = sums[spot(-6)].astype(F32) + arrived(legs[-7], legs[-5])
-        six[1] = sums[spot(6)].astype(F32) + arrived(legs[7], legs[5])
-        six[c] += arrived(legs[8])
-        for i, o in enumerate((-6, 6)):
-            passed[i] = six[i].astype(BF16)
-            slots[0] += 1
-            slot = came.at[slots[0] - 1]
-            legs[o] = (slots[0] - 1, send(passed.at[i], slot, (0, 0, -3 if o < 0 else 3, 0)))
+        def from_here(legs, rows):
+            return sum(came[leg[0], rows].astype(F32) for leg in legs)
+
+        landed([legs[o][1] for o in (-7, -5, 7, 5, 8)])
+        for h, rows in enumerate(HALVES):
+            six[0, rows] = sums[spot(-6), rows].astype(F32) + from_here((legs[-7], legs[-5]), rows)
+            six[1, rows] = sums[spot(6), rows].astype(F32) + from_here((legs[7], legs[5]), rows)
+            six[c, rows] += came[legs[8][0], rows].astype(F32)
+            for i, o in enumerate((-6, 6)):
+                passed[i, rows] = six[i, rows].astype(BF16)
+                copy = send(passed.at[i, rows], came.at[11 + i, rows], (0, 0, o // 2, 0))
+                legs[o, h] = (11 + i, copy)
         meanwhile()
-        for i, s in enumerate((-1, 1)):
-            three = sums[spot(3 * s)].astype(F32) + arrived(legs[2 * s], legs[4 * s]) + arrived(legs[6 * s])
-            passed[2 + i] = three.astype(BF16)
-            slots[0] += 1
-            slot = came.at[slots[0] - 1]
-            legs[3 * s] = (slots[0] - 1, send(passed.at[2 + i], slot, (0, 0, 3 * s, 0)))
-        total = sums[z].astype(F32) + arrived(legs[-1], legs[1])
-        return total + arrived(legs[-3], legs[3])
+        landed([legs[o][1] for o in (-4, -2, 4, 2)])
+        for h, rows in enumerate(HALVES):
+            for i, s in enumerate((-1, 1)):
+                landed([legs[6 * s, h][1]])
+                three = sums[spot(3 * s), rows].astype(F32)
+                three += from_here((legs[2 * s], legs[4 * s], legs[6 * s, h]), rows)
+                passed[2 + i, rows] = three.astype(BF16)
+                copy = send(passed.at[2 + i, rows], came.at[13 + i, rows], (0, 0, 3 * s, 0))
+                legs[3 * s, h] = (13 + i, copy)
+        landed([legs[-1][1], legs[1][1]])
+        landed([legs[3 * s, h][1] for s in (-1, 1) for h in range(2)])
+        total = sums[z].astype(F32)
+        for leg in (9, 10, 13, 14):
+            total += came[leg].astype(F32)
+        return total
 
     late = {}
 

time: 142 us -> 139 us (0.979)
  Pallas kernels: 140 us -> 137 us
    pallas_call x1, Pallas kernels: 140 us -> 137 us  [local(): pl.pallas_call(kernel, out_shape=jax.ShapeDtypeStruct((FEAT, TOK), BF16),...]
where the time goes in v4:
time: 139 us; the launch traced here: 138 us
  Pallas kernels  137 us (99%)
  local copies, waits for them, and re-layouts  1.4 us (1%)
    pallas_call x1, Pallas kernels, local(): pl.pallas_call(kernel, out_shape=jax.ShapeDtypeStruct((FEAT, TOK), BF16),...  137 us

profile of v4, /device:TPU:1, one launch (start us, length us, event | category | flops | bytes accessed | tf_op | source)
XLA Modules:
  0.0 137.9 jit_solution(8283298420851930508)
XLA Ops:
  0.0 136.5 %shard_map.136 = bf16[160,128]{1,0:T(8,128)(2,1)} custom-call(bf16[160,128]{1,0:T(8,128)(2,1)} %bitcast.5, f32[2560]{0:T(1024)} %first_gain_ref.1, bf16[80,512]{1,0:T(8,128)(2,1)} %dense_gate_ref.1, bf16[80,512]{1,0:T(8,128)(2,1)} %dense_up_ref.1, bf16[80,512]{1,0:T(8,128)(2,1)} %dense_down_ref.1, f32[2560]{0:T(1024)} %second_gain_ref.1, ...), custom_call_target="tpu_custom_call" | custom-call | tf_op jit(solution)/shard_map/pallas_call | solution.py:528
  136.5 1.4 %copy.16 = bf16[128,160]{0,1:T(8,128)(2,1)} copy(bf16[128,160]{0,1:T(8,128)(2,1)} %bitcast.4) | data formatting | bytes 81920
